TPU v7x, 128 devices: a whole 4x4x4 slice. The times are simulated.
128 devices in a mesh: aperture: 16 (over x_hi, z, core), range: 8 (over y, x_lo).
Axes of the slice: x: 4 (x_hi: 2, x_lo: 2; x = x_hi * 2 + x_lo), y: 4, z: 4, core: 2. Of those that a mesh axis runs over, the one named last changes fastest.
Arguments:
- child_image: float32 [2, 4096, 8192], P(None, 'aperture', 'range'), may hold values from -6 to 6
- tap_weights: float32 [4, 2, 4, 4096], P(None, None, None, 'aperture'), may hold values from -3 to 3
- band_offsets: int32 [4, 2, 4096], P(None, None, 'aperture'), may hold values from 0 to 252, as said below
- range_shift: float32 [4, 2, 4096], P(None, None, 'aperture'), may hold values from -1 to 1
- phase_base: float32 [4, 2, 4096], P(None, None, 'aperture'), may hold values from -3.140625 to 3.140625
- phase_slope: float32 [4, 2, 4096], P(None, None, 'aperture'), may hold values from -6 to 6
- tile_sources: int32 [16, 8], P('aperture'), may hold values from 0 to 15, as said below
- tile_counts: int32 [16], P('aperture'), may hold values from 1 to 8
- resample_weights: bfloat16 [16, 8, 512, 256], P('aperture'), may hold values from -0.1875 to 0.1875
Outputs:
- ground_image: float32 [2, 8192, 8192], P(None, 'aperture', 'range')
Inputs may be any that keep to these rules, and one draw needn't show every extreme that they name: band_offsets[l, s, a * 256 + q] lies between h * 128 and h * 128 + 256 / 2 - 4, where h is bit l of a; both ends are reached. `tile_sources`: the first tile_counts[g] entries of row g are different beam blocks; entries past the count are ignored; some tile lists 8 blocks.
All inputs are finite; a program needn't handle non-finite values.
Results may differ from a plain program's by a relative error of at most 0.0029.
Values may be sent and summed in bfloat16 or wider, within the bound.
A program may use at most 128 MiB of HBM per device.

v0:
```python
import jax
import jax.numpy as jnp
from jax import lax
from jax.sharding import PartitionSpec as P

RANGE = 8192


merge_scale = 0.70710678


def with_halo(cells, sides, width):
    for axis, dim in sides:
        count = lax.axis_size(axis)
        ends = count - 1
        head = lax.slice_in_dim(cells, 0, width, axis=dim)
        tail = lax.slice_in_dim(cells, cells.shape[dim] - width, cells.shape[dim], axis=dim)
        cells = jnp.concatenate(
            [
                lax.ppermute(tail, axis, [(i, (i + 1) % count) for i in range(ends)]),
                cells,
                lax.ppermute(head, axis, [((i + 1) % count, i) for i in range(ends)]),
            ],
            axis=dim,
        )
    return cells


def from_partner(value, axis, distance):
    mask = 2**distance
    pairs = [(source, source ^ mask) for source in range(lax.axis_size(axis))]
    return lax.ppermute(value, axis, pairs)


def beam_interp(child_rows, offsets, weights):
    tap_index = jnp.arange(weights.shape[0], dtype=jnp.int32)
    row_index = offsets[None, :] + tap_index[:, None]
    picked = child_rows[:, row_index, :]
    return jnp.sum(picked * weights[None, :, :, None], axis=1)


def finish_side(beam_part, shifts, base_phase, slope_phase, radius):
    center = beam_part[:, :, 1:-1]
    range_next = beam_part[:, :, 2:]
    range_prev = beam_part[:, :, :-2]
    shifts = shifts[:, None]
    shifted = (
        center
        + jnp.maximum(shifts, 0.0) * (range_next - center)
        + jnp.maximum(-shifts, 0.0) * (range_prev - center)
    )
    angles = base_phase[:, None] + slope_phase[:, None] * radius[None, :]
    cosine = jnp.cos(angles)
    sine_part = jnp.sin(angles)
    real_part = shifted[0] * cosine - shifted[1] * sine_part
    imag_part = shifted[0] * sine_part + shifted[1] * cosine
    return jnp.stack([real_part, imag_part])


def shards(
    child_image,
    tap_weights,
    band_offsets,
    range_shift,
    phase_base,
    phase_slope,
    tile_sources,
    tile_counts,
    resample_weights,
):
    beams_dev = child_image.shape[1]
    range_dev = child_image.shape[2]
    range_first = lax.axis_index("range") * range_dev
    radius = (range_first + jnp.arange(range_dev, dtype=jnp.int32)).astype(jnp.float32) / RANGE
    position = lax.axis_index("aperture")
    current = child_image
    for merge_level in range(lax.axis_size("aperture").bit_length() - 1):
        half_bit = jnp.bitwise_and(jnp.right_shift(position, merge_level), 1)
        extended = with_halo(current, (("range", 2),), 1)
        received = from_partner(extended, "aperture", merge_level)
        keep_own = half_bit == 0
        lower_child = jnp.where(keep_own, extended, received)
        upper_child = jnp.where(keep_own, received, extended)
        parent = jnp.zeros((2, beams_dev, range_dev), jnp.float32)
        for child_side, child_rows in ((0, lower_child), (1, upper_child)):
            offsets = band_offsets[merge_level, child_side]
            beam_part = beam_interp(child_rows, offsets, tap_weights[merge_level, child_side])
            parent = parent + finish_side(
                beam_part,
                range_shift[merge_level, child_side],
                phase_base[merge_level, child_side],
                phase_slope[merge_level, child_side],
                radius,
            )
        current = parent * merge_scale
    polar_image = current.astype(jnp.bfloat16)
    sources = tile_sources[0]
    live_count = tile_counts[0]
    matrices = resample_weights[0]
    slot_ids = jnp.arange(sources.shape[0], dtype=jnp.int32)
    starting = jnp.zeros((2, matrices.shape[1], range_dev), jnp.float32)
    gathered_piece = lax.all_gather(polar_image, "aperture", axis=1, tiled=True)
    block_count = gathered_piece.shape[1] // beams_dev

    def add_one(block_slot, summed):
        block_image = lax.dynamic_slice_in_dim(gathered_piece, block_slot * beams_dev, beams_dev, 1)
        matches = (sources == block_slot) & (slot_ids < live_count)
        slot_pos = jnp.argmax(matches.astype(jnp.int32))

        def product():
            matrix = lax.dynamic_index_in_dim(matrices, slot_pos, 0, keepdims=False)
            return summed + jnp.einsum(
                "cb,xbr->xcr", matrix, block_image, preferred_element_type=jnp.float32
            )

        def unchanged():
            return summed

        return lax.cond(jnp.any(matches), product, unchanged)

    return lax.fori_loop(0, block_count, add_one, starting)


def solution(mesh):
    placed = (
        P(None, "aperture", "range"),
        P(None, None, None, "aperture"),
        P(None, None, "aperture"),
        P(None, None, "aperture"),
        P(None, None, "aperture"),
        P(None, None, "aperture"),
        P("aperture", None),
        P("aperture"),
        P("aperture", None, None, None),
    )
    return jax.shard_map(
        shards, mesh=mesh, in_specs=placed, out_specs=P(None, "aperture", "range"), check_vma=False
    )
```

profile of v0, /device:TPU:1, one launch (start us, length us, event | category | flops | bytes accessed | tf_op | source)
XLA Modules:
  0.0 845.8 jit_solution(7733100293309067517)
XLA Ops:
  6.5 3.2 copy.53
  11.4 4.0 collective-permute-start
  16.7 3.6 collective-permute-done
  20.3 7.6 collective-permute-done.1
  28.0 8.4 concatenate.12
  36.4 3.4 copy.56
  42.0 3.9 collective-permute-done.2
  45.9 5.1 copy.57
  51.0 4.1 broadcast_select_fusion
  55.1 20.7 %gather_fusion = f32[1024,2,1026]{2,1,0:T(2,128)} fusion(f32[2,256,1026]{2,0,1:T(2,128)} %bitcast.134, s32[1024]{0:T(1024)S(1)} %broadcast_clamp_fusion.7), kind=kCustom, calls=%fused_computation | custom fusion | bytes 16814080 | tf_op jit(solution)/shard_map/gather | solution.py:38
  75.8 10.4 %multiply_reduce_fusion.7 = f32[256,2,1026]{2,1,0:T(2,128)S(1)} fusion(f32[4,256,2,1026]{3,2,1,0:T(2,128)} %bitcast.137, f32[4,256]{1,0:T(4,128)S(1)} %get-tuple-element.283), kind=kLoop, calls=%fused_computation.24 | loop fusion | flops 3677184 | bytes 10510336 | tf_op jit(solution)/shard_map/reduce_sum | solution.py:39
  87.8 19.0 %gather_fusion.1 = f32[1024,2,1026]{2,1,0:T(2,128)} fusion(f32[2,256,1026]{2,0,1:T(2,128)S(1)} %bitcast.133, s32[1024]{0:T(1024)S(1)} %broadcast_clamp_fusion.6), kind=kCustom, calls=%fused_computation.1 | custom fusion | bytes 16814080 | tf_op jit(solution)/shard_map/gather | solution.py:38
  106.7 10.4 %multiply_reduce_fusion.6 = f32[256,2,1026]{2,1,0:T(2,128)S(1)} fusion(f32[4,256,2,1026]{3,2,1,0:T(2,128)} %bitcast.138, f32[4,256]{1,0:T(4,128)S(1)} %get-tuple-element.282), kind=kLoop, calls=%fused_computation.23 | loop fusion | flops 3677184 | bytes 10510336 | tf_op jit(solution)/shard_map/reduce_sum | solution.py:39
  121.2 18.6 %multiply_subtract_fusion.6 = (f32[1,256,1024]{2,1,0:T(8,128)S(1)}, f32[1,256,1024]{2,1,0:T(8,128)S(1)}, f32[1,256,1024]{2,1,0:T(8,128)S(1)}, f32[1,256,1024]{2,1,0:T(8,128)S(1)}) fusion(f32[2,256,1024]{2,1,0:T(8,128)S(1)} %fusion.32, f32[256]{0:T(256)S(1)} %bitcast.189, f32[256]{0:T(256)S(1)} %bitcast.187, f32[1024]{0:T(1024)S(1)} %convert_multiply_fusion, ...), kind=kLoop, calls=%fused_computation.129 | loop fusion | flops 4194304 | bytes 8396800 | tf_op jit(solution)/shard_map/sub | solution.py:55
  140.4 3.1 collective-permute-start.3
  144.9 4.0 collective-permute-done.3
  148.8 7.6 collective-permute-done.4
  156.5 3.1 concatenate.13
  164.2 45.0 %collective-permute-done.5 = f32[2,256,1026]{1,0,2:T(2,128)} collective-permute-done((f32[2,256,1026]{1,0,2:T(2,128)}, f32[2,256,1026]{1,0,2:T(2,128)}, u32[]{:S(2)}, u32[]{:S(2)}) %collective-permute-start.5) | collective-permute-done | bytes 2101280 | tf_op jit(solution)/shard_map/ppermute | solution.py:32
  209.2 4.6 copy.62
  213.7 3.4 broadcast_select_fusion.2
  218.9 19.0 %gather_fusion.2 = f32[1024,2,1026]{2,1,0:T(2,128)} fusion(f32[2,256,1026]{2,0,1:T(2,128)S(1)} %copy.63, s32[1024]{0:T(1024)S(1)} %broadcast_clamp_fusion.5), kind=kCustom, calls=%fused_computation.2 | custom fusion | bytes 16814080 | tf_op jit(solution)/shard_map/gather | solution.py:38
  237.9 10.4 %multiply_reduce_fusion.5 = f32[256,2,1026]{2,1,0:T(2,128)S(1)} fusion(f32[4,256,2,1026]{3,2,1,0:T(2,128)} %bitcast.139, f32[4,256]{1,0:T(4,128)S(1)} %get-tuple-element.281), kind=kLoop, calls=%fused_computation.22 | loop fusion | flops 3677184 | bytes 10510336 | tf_op jit(solution)/shard_map/reduce_sum | solution.py:39
  252.7 19.0 %gather_fusion.3 = f32[1024,2,1026]{2,1,0:T(2,128)} fusion(f32[2,256,1026]{2,0,1:T(2,128)S(1)} %copy.66, s32[1024]{0:T(1024)S(1)} %broadcast_clamp_fusion.4), kind=kCustom, calls=%fused_computation.3 | custom fusion | bytes 16814080 | tf_op jit(solution)/shard_map/gather | solution.py:38
  271.7 10.6 %multiply_reduce_fusion.4 = f32[256,2,1026]{2,1,0:T(2,128)S(1)} fusion(f32[4,256,2,1026]{3,2,1,0:T(2,128)} %bitcast.140, f32[4,256]{1,0:T(4,128)S(1)} %get-tuple-element.280), kind=kLoop, calls=%fused_computation.21 | loop fusion | flops 3677184 | bytes 10510336 | tf_op jit(solution)/shard_map/reduce_sum | solution.py:39
  286.4 8.2 multiply_subtract_fusion.4
  295.2 3.1 collective-permute-start.6
  302.0 7.3 collective-permute-done.7
  315.3 3.1 collective-permute-start.8
  318.5 43.2 %collective-permute-done.8 = f32[2,256,1026]{1,0,2:T(2,128)} collective-permute-done((f32[2,256,1026]{1,0,2:T(2,128)}, f32[2,256,1026]{1,0,2:T(2,128)}, u32[]{:S(2)}, u32[]{:S(2)}) %collective-permute-start.8) | collective-permute-done | bytes 2101280 | tf_op jit(solution)/shard_map/ppermute | solution.py:32
  361.7 5.0 copy.69
  366.7 3.4 broadcast_select_fusion.4
  371.9 19.0 %gather_fusion.4 = f32[1024,2,1026]{2,1,0:T(2,128)} fusion(f32[2,256,1026]{2,0,1:T(2,128)S(1)} %copy.70, s32[1024]{0:T(1024)S(1)} %broadcast_clamp_fusion.3), kind=kCustom, calls=%fused_computation.4 | custom fusion | bytes 16814080 | tf_op jit(solution)/shard_map/gather | solution.py:38
  390.9 10.4 %multiply_reduce_fusion.3 = f32[256,2,1026]{2,1,0:T(2,128)S(1)} fusion(f32[4,256,2,1026]{3,2,1,0:T(2,128)} %bitcast.141, f32[4,256]{1,0:T(4,128)S(1)} %get-tuple-element.279), kind=kLoop, calls=%fused_computation.20 | loop fusion | flops 3677184 | bytes 10510336 | tf_op jit(solution)/shard_map/reduce_sum | solution.py:39
  405.6 19.0 %gather_fusion.5 = f32[1024,2,1026]{2,1,0:T(2,128)} fusion(f32[2,256,1026]{2,0,1:T(2,128)S(1)} %copy.73, s32[1024]{0:T(1024)S(1)} %broadcast_clamp_fusion.2), kind=kCustom, calls=%fused_computation.5 | custom fusion | bytes 16814080 | tf_op jit(solution)/shard_map/gather | solution.py:38
  424.6 10.6 %multiply_reduce_fusion.2 = f32[256,2,1026]{2,1,0:T(2,128)S(1)} fusion(f32[4,256,2,1026]{3,2,1,0:T(2,128)} %bitcast.142, f32[4,256]{1,0:T(4,128)S(1)} %get-tuple-element.278), kind=kLoop, calls=%fused_computation.19 | loop fusion | flops 3677184 | bytes 10510336 | tf_op jit(solution)/shard_map/reduce_sum | solution.py:39
  439.3 8.2 multiply_subtract_fusion.2
  449.4 4.0 collective-permute-start.9
  465.8 39.9 %collective-permute-done.11 = f32[2,256,1026]{1,0,2:T(2,128)} collective-permute-done((f32[2,256,1026]{1,0,2:T(2,128)}, f32[2,256,1026]{1,0,2:T(2,128)}, u32[]{:S(2)}, u32[]{:S(2)}) %collective-permute-start.11) | collective-permute-done | bytes 2101280 | tf_op jit(solution)/shard_map/ppermute | solution.py:32
  505.7 4.8 copy.76
  514.3 3.2 copy.80
  517.5 18.9 %gather_fusion.6 = f32[1024,2,1026]{2,1,0:T(2,128)} fusion(f32[2,256,1026]{2,0,1:T(2,128)S(1)} %copy.77, s32[1024]{0:T(1024)S(1)} %broadcast_clamp_fusion.1), kind=kCustom, calls=%fused_computation.6 | custom fusion | bytes 16814080 | tf_op jit(solution)/shard_map/gather | solution.py:38
  536.3 20.7 %gather_fusion.7 = f32[1024,2,1026]{2,1,0:T(2,128)} fusion(f32[2,256,1026]{2,0,1:T(2,128)} %copy.80, s32[1024]{0:T(1024)S(1)} %broadcast_clamp_fusion), kind=kCustom, calls=%fused_computation.7 | custom fusion | bytes 16814080 | tf_op jit(solution)/shard_map/gather | solution.py:38
  557.1 16.0 %multiply_reduce_fusion = (f32[256,2,1026]{2,1,0:T(2,128)S(1)}, f32[256,2,1026]{2,1,0:T(2,128)S(1)}) fusion(f32[4,256,2,1026]{3,2,1,0:T(2,128)} %bitcast.136, f32[4,256]{1,0:T(4,128)S(1)} %get-tuple-element.277, f32[4,256,2,1026]{3,2,1,0:T(2,128)} %bitcast.135, f32[4,256]{1,0:T(4,128)S(1)} %get-tuple-element.284), kind=kLoop, calls=%fused_computation.17 | loop fusion | flops 7354368 | bytes 21020672 | tf_op jit(solution)/shard_map/reduce_sum | solution.py:39
  575.8 8.2 multiply_subtract_fusion
  586.7 124.0 %all-gather.2.cloned.1.call-done = bf16[2,4096,1024]{2,0,1:T(2,128)(2,1)} async-done(((bf16[2,256,1024]{2,0,1:T(2,128)(2,1)}), bf16[2,4096,1024]{2,0,1:T(2,128)(2,1)}) %all-gather.2.cloned.1.call-update) | async-done | bytes 16777232 | tf_op jit(solution)/shard_map/all_gather | solution.py:102
  710.7 16.4 %copy.83 = bf16[2,4096,1024]{2,1,0:T(8,128)(2,1)} copy(bf16[2,4096,1024]{2,0,1:T(2,128)(2,1)} %all-gather.2.cloned.1.call-done) | data formatting | bytes 33554432
  729.6 109.0 %while.17 = (s32[]{:T(128)}, f32[2,512,1024]{2,1,0:T(8,128)}, s32[8]{0:T(128)S(1)}, s32[]{:T(128)}, bf16[8,512,256]{2,1,0:T(8,128)(2,1)}, /*index=5*/bf16[2,4096,1024]{2,1,0:T(8,128)(2,1)}, s32[]{:T(128)}) while((s32[]{:T(128)}, f32[2,512,1024]{2,1,0:T(8,128)}, s32[8]{0:T(128)S(1)}, s32[]{:T(128)}, ...), condition=%wide.region_13.14_spmd.clone, body=%wide.region_8.13_spmd.clone.sunk | while | flops 537919616 | bytes 9699635 | solution.py:121
  732.9 7.0 conditional.3
  734.6 5.3 bitcast_add_fusion
  743.2 7.0 conditional.3
  744.9 5.3 bitcast_add_fusion
  753.6 7.0 conditional.3
  755.3 5.3 bitcast_add_fusion
  763.9 7.0 conditional.3
  765.6 5.3 bitcast_add_fusion
  774.2 7.0 conditional.3
  775.9 5.3 bitcast_add_fusion
  784.5 7.0 conditional.3
  786.2 5.3 bitcast_add_fusion
  794.8 7.0 conditional.3
  796.5 5.3 bitcast_add_fusion
  831.6 7.0 conditional.3
  833.3 5.3 bitcast_add_fusion
  (151 shorter events, 116.2 us)
Async XLA Ops:
  6.5 704.1 %all-gather.2.cloned.1.call-start = ((), (), s32[]{:S(2)}) async-start(), calls=%async_computation | async-start | bytes 17825792 | tf_op jit(solution)/shard_map/all_gather | solution.py:102
  9.7 1.3 copy-start.7
  11.4 8.9 %collective-permute-start = (f32[2,256,1]{2,0,1:T(2,128)S(1)}, f32[2,256,1]{2,0,1:T(2,128)S(1)}, u32[]{:S(2)}, u32[]{:S(2)}) collective-permute-start(f32[2,256,1]{2,0,1:T(2,128)S(1)} %get-tuple-element.276), channel_id=1, source_target_pairs={{0,1},{1,2},{2,3},{3,4},{4,5},{5,6},{6,7},{8,9},{9,10},{10,11},{11... | collective-permute-start | bytes 6152 | tf_op jit(solution)/shard_map/ppermute | solution.py:20
  15.4 12.6 %collective-permute-start.1 = (f32[2,256,1]{2,0,1:T(2,128)S(1)}, f32[2,256,1]{2,0,1:T(2,128)S(1)}, u32[]{:S(2)}, u32[]{:S(2)}) collective-permute-start(f32[2,256,1]{2,0,1:T(2,128)S(1)} %get-tuple-element.275), channel_id=1, source_target_pairs={{1,0},{2,1},{3,2},{4,3},{5,4},{6,5},{7,6},{9,8},{10,9},{11,10},{12... | collective-permute-start | bytes 6152 | tf_op jit(solution)/shard_map/ppermute | solution.py:22
  36.3 3.5 copy-start.3
  36.4 5.4 copy-start.13
  36.4 5.5 copy-start.14
  36.4 5.5 copy-start.15
  36.4 5.5 copy-start.12
  36.4 5.5 copy-start.11
  39.8 6.0 collective-permute-start.2
  117.1 1.7 copy-start.2
  140.3 8.6 %copy-start.4 = (f32[2,256,1024]{2,1,0:T(8,128)}, f32[2,256,1024]{2,1,0:T(8,128)S(1)}, u32[]{:S(2)}) copy-start(f32[2,256,1024]{2,1,0:T(8,128)S(1)} %fusion.39) | copy-start | bytes 6291460
  140.4 8.4 collective-permute-start.3
  143.6 12.9 %collective-permute-start.4 = (f32[2,256,1]{2,1,0:T(8,128)S(1)}, f32[2,256,1]{2,1,0:T(8,128)S(1)}, u32[]{:S(2)}, u32[]{:S(2)}) collective-permute-start(f32[2,256,1]{2,1,0:T(8,128)S(1)} %get-tuple-element.273), channel_id=1, source_target_pairs={{1,0},{2,1},{3,2},{4,3},{5,4},{6,5},{7,6},{9,8},{10,9},{11,10},{12... | collective-permute-start | bytes 6152 | tf_op jit(solution)/shard_map/ppermute | solution.py:22
  162.5 46.7 %collective-permute-start.5 = (f32[2,256,1026]{1,0,2:T(2,128)}, f32[2,256,1026]{1,0,2:T(2,128)}, u32[]{:S(2)}, u32[]{:S(2)}) collective-permute-start(f32[2,256,1026]{1,0,2:T(2,128)} %copy.61), channel_id=1, source_target_pairs={{0,16},{8,24},{16,0},{24,8},{32,48},{40,56},{48,32},{56,40},{64,80... | collective-permute-start | bytes 6303752 | tf_op jit(solution)/shard_map/ppermute | solution.py:32
  248.3 2.5 copy-start.8
  282.3 1.7 copy-start
  295.1 6.9 copy-start.5
  295.2 6.7 collective-permute-start.6
  298.4 10.9 %collective-permute-start.7 = (f32[2,256,1]{2,1,0:T(8,128)S(1)}, f32[2,256,1]{2,1,0:T(8,128)S(1)}, u32[]{:S(2)}, u32[]{:S(2)}) collective-permute-start(f32[2,256,1]{2,1,0:T(8,128)S(1)} %get-tuple-element.271), channel_id=1, source_target_pairs={{1,0},{2,1},{3,2},{4,3},{5,4},{6,5},{7,6},{9,8},{10,9},{11,10},{12... | collective-permute-start | bytes 6152 | tf_op jit(solution)/shard_map/ppermute | solution.py:22
  315.3 46.4 %collective-permute-start.8 = (f32[2,256,1026]{1,0,2:T(2,128)}, f32[2,256,1026]{1,0,2:T(2,128)}, u32[]{:S(2)}, u32[]{:S(2)}) collective-permute-start(f32[2,256,1026]{1,0,2:T(2,128)} %copy.68), channel_id=1, source_target_pairs={{0,32},{8,40},{16,48},{24,56},{32,0},{40,8},{48,16},{56,24},{64,96... | collective-permute-start | bytes 6303752 | tf_op jit(solution)/shard_map/ppermute | solution.py:32
  401.3 2.5 copy-start.9
  435.2 1.7 copy-start.1
  448.0 7.3 copy-start.6
  448.1 7.1 collective-permute-start.10
  449.4 7.3 collective-permute-start.9
  462.8 42.9 %collective-permute-start.11 = (f32[2,256,1026]{1,0,2:T(2,128)}, f32[2,256,1026]{1,0,2:T(2,128)}, u32[]{:S(2)}, u32[]{:S(2)}) collective-permute-start(f32[2,256,1026]{1,0,2:T(2,128)} %copy.75), channel_id=1, source_target_pairs={{0,64},{8,72},{16,80},{24,88},{32,96},{40,104},{48,112},{56,120},{... | collective-permute-start | bytes 6303752 | tf_op jit(solution)/shard_map/ppermute | solution.py:32
  727.1 2.5 copy-start.10
Sparse Core Ops, SparseCore 0:
  586.8 123.7 all-gather.1
where the time goes:
time: 852 us; the launch traced here: 846 us
  waiting for transfers between devices  292 us (34%)
  local copies, waits for them, and re-layouts  255 us (30%)
  other arithmetic  189 us (22%)
  matrix products  42.7 us (5%)
  starting transfers between devices  29 us (3%)
  loops' own time  23.9 us (3%)
  between operations  14.3 us (2%)
    gather x8, local copies, waits for them, and re-layouts, beam_interp(): picked = child_rows[:, row_index, :]  155 us
    ppermute x4, waiting for transfers between devices, from_partner(): return lax.ppermute(value, axis, pairs)  132 us
    all_gather x1, waiting for transfers between devices, shards(): gathered_piece = lax.all_gather(polar_image, 'aperture', axis=1, tiled=True)  124 us
    reduce_sum x7, other arithmetic, beam_interp(): return jnp.sum(picked * weights[None, :, :, None], axis=1)  78.7 us
    sub x4, other arithmetic, finish_side(): real_part = shifted[0] * cosine - shifted[1] * sine_part  43.3 us
    dot_general x8, matrix products, product(): jnp.einsum('cb,xbr->xcr', matrix, block_image, preferred_element_type=jnp...  42.7 us
    concatenate x8, local copies, waits for them, and re-layouts, with_halo(): jnp.concatenate([lax.ppermute(tail, axis, [(i, (i + 1) % count) for i in...  29.9 us
    unnamed x42, local copies, waits for them, and re-layouts  27.5 us
  transfers between devices with their start and end apart: 13, of which 13 were waited for; matrix products, arithmetic and copies ran while one was open for 0% of the time, Pallas kernels for 0%

commit v1 on v0

v1 whole, which is shorter than its diff:
```python
import functools

import jax
import jax.numpy as jnp
from jax import lax
from jax.experimental import pallas as pl
from jax.experimental.pallas import tpu as pltpu
from jax.sharding import PartitionSpec as P

RANGE = 8192
SCALE = 0.70710678
MESH = pl.DeviceIdType.MESH
SUBS = 2
ROWS = 64
TILES = 9
F32 = jnp.float32
BF16 = jnp.bfloat16


def kernel(
    child, taps, bands, shifts, bases, slopes, sources_v, counts_v, matrices, sources, counts,
    out,
    staged, edges, received, split, part, bank, wave, rates, own_par, par,
    g00, g01, g10, g11, g20, g21, g30, g31,
    other_mat, wide, columns, sent_tiles, got_tiles, held, info, info_got, info_s,
    a2a_send, a2a_recv, edge_send, edge_recv, par_send, par_recv, pary_send, pary_recv,
    mat_send, mat_recv, maty_send, maty_recv, ring_send, ring_recv, relay_send, relay_recv,
    core_send, core_recv, tile_send, tile_recv, info_send, info_recv, local_sem,
):
    gathered = ((g00, g01), (g10, g11), (g20, g21), (g30, g31))
    a = lax.axis_index("aperture")
    p = lax.axis_index("range")
    core, z, xh = a % 2, (a // 2) % 4, a // 8
    y, xl = p // 2, p % 2
    me = a // 2
    sibling = (me * 2 + 1 - core, p)
    z_next = (xh * 8 + ((z + 1) % 4) * 2 + core, p)
    z_prev = (xh * 8 + ((z + 3) % 4) * 2 + core, p)
    x_pair = ((a + 8) % 16, p)
    x_side = ((a + 8) % 16, y * 2 + 1 - xl)
    r_next = (a, (p + 1) % 8)
    r_prev = (a, (p + 7) % 8)

    def y_peer(step):
        return (a, ((y + step) % 4) * 2 + xl)

    barrier = pltpu.get_barrier_semaphore()

    def greet(step, carry):
        pl.semaphore_signal(barrier, inc=1, device_id=((a + step) % 16, p), device_id_type=MESH)
        return carry

    lax.fori_loop(1, 16, greet, 0)
    for peer in (x_side, r_next, r_prev, y_peer(1), y_peer(2), y_peer(3)):
        pl.semaphore_signal(barrier, inc=1, device_id=peer, device_id_type=MESH)

    for level in range(4):
        for side in range(2):
            row = side * 8
            own_par[level, row : row + 4, :] = taps[level, side]
            own_par[level, row + 4 : row + 5, :] = bands[level, side : side + 1, :].astype(F32)
            own_par[level, row + 5 : row + 6, :] = shifts[level, side : side + 1, :]
            own_par[level, row + 6 : row + 7, :] = bases[level, side : side + 1, :]
            own_par[level, row + 7 : row + 8, :] = slopes[level, side : side + 1, :]
    info[...] = jnp.zeros((8, 128), jnp.int32)
    info[0:1, 0:8] = sources_v[...]
    info[1:2, 0:1] = counts_v[...]

    pl.semaphore_wait(barrier, 21)

    def remote(src, dst, send, recv, to):
        return pltpu.make_async_remote_copy(
            src_ref=src, dst_ref=dst, send_sem=send, recv_sem=recv, device_id=to, device_id_type=MESH
        )

    def par_copy(step, slot):
        return remote(
            own_par.at[y], par.at[y, slot], par_send.at[step], par_recv.at[slot], ((a + 2 * step) % 16, p)
        )

    def send_par(step, carry):
        par_copy(step, me).start()
        return carry

    lax.fori_loop(1, 8, send_par, 0)
    mat_copy = remote(
        matrices.at[pl.ds(2 * y, 2)], other_mat.at[pl.ds(2 * y, 2)], mat_send.at[0], mat_recv.at[0], x_side
    )
    mat_copy.start()
    info_copy = remote(info, info_got, info_send.at[0], info_recv.at[0], x_pair)
    info_copy.start()

    def turn(k, carry):
        for comp in range(2):
            for half in range(2):
                block = child[comp, half * 128 : half * 128 + 128, pl.ds(pl.multiple_of(k * 128, 128), 128)]
                block = block.T.reshape(2, 8, 8, 128)
                for sub in range(2):
                    staged[k * 2 + sub, half, 0:8, comp] = block[sub]
        return carry

    lax.fori_loop(0, 8, turn, 0)
    edge_next = remote(staged.at[15, :, 7], edges.at[0], edge_send.at[0], edge_recv.at[0], r_next)
    edge_prev = remote(staged.at[0, :, 0], edges.at[1], edge_send.at[1], edge_recv.at[1], r_prev)
    edge_next.start()
    edge_prev.start()
    low = lax.broadcasted_iota(jnp.int32, (8, 128), 0) < 4

    def fill(j, carry):
        for half in range(2):
            for comp in range(2):
                staged[j, half, 8, comp] = jnp.where(low, staged[j + 1, half, 0, comp], staged[j - 1, half, 7, comp])
        return carry

    lax.fori_loop(1, 15, fill, 0)
    edge_next.wait()
    edge_prev.wait()
    has_prev = jnp.where(p > 0, 1.0, 0.0).astype(F32)
    has_next = jnp.where(p < 7, 1.0, 0.0).astype(F32)
    for half in range(2):
        for comp in range(2):
            staged[0, half, 8, comp] = jnp.where(low, staged[1, half, 0, comp], edges[0, half, comp] * has_prev)
            staged[15, half, 8, comp] = jnp.where(low, edges[1, half, comp] * has_next, staged[14, half, 7, comp])

    def child_copy(sub, step, slot):
        to = (a + step) % 16
        return remote(
            staged.at[(to // 2) * 2 + sub, to % 2],
            received.at[sub, slot],
            a2a_send.at[sub, step],
            a2a_recv.at[sub, slot],
            (to, p),
        )

    for sub in range(SUBS):

        def send_child(step, carry, sub=sub):
            child_copy(sub, step, a).start()
            return carry

        lax.fori_loop(1, 16, send_child, 0)
        pltpu.make_async_copy(staged.at[me * 2 + sub, core], received.at[sub, a], local_sem.at[sub]).start()

    par[y, me] = own_par[y]

    def wait_par(step, carry):
        par_copy(step, (me + step) % 8).wait_recv()
        return carry

    lax.fori_loop(1, 8, wait_par, 0)

    def pary_copy(step):
        return remote(par.at[y], par.at[y], pary_send.at[step], pary_recv.at[step], y_peer(step))

    def pary_wait(step):
        there = (y + 4 - step) % 4
        remote(par.at[there], par.at[there], pary_send.at[step], pary_recv.at[step], y_peer(step)).wait_recv()

    for step in (1, 2, 3):
        pary_copy(step).start()
    for step in (1, 2, 3):
        pary_wait(step)

    first = p * 1024 + me * (SUBS * ROWS)
    beam = lax.broadcasted_iota(jnp.int32, (128, 256), 0).astype(F32)
    radius = (first + lax.broadcasted_iota(jnp.int32, (8, 256), 0)).astype(F32) * (1.0 / RANGE)
    for level in range(4):

        def prepare(q, carry, level=level):
            half = core if level == 0 else (q // (1 << (level - 1))) % 2
            start = (half * 128).astype(F32)
            for side in range(2):
                index = (level * 8 + q) * 2 + side
                rows = par[level, q, side * 8 : side * 8 + 8, :]
                offset = beam - (rows[4:5] - start)
                banded = jnp.zeros((128, 256), F32)
                for tap in range(4):
                    banded = jnp.where(offset == float(tap), rows[tap : tap + 1], banded)
                high = banded.astype(BF16)
                bank[index, 0:128] = high
                bank[index, 128:256] = (banded - high.astype(F32)).astype(BF16)
                angle = rows[6:7] + rows[7:8] * radius
                wave[index, 0] = SCALE * jnp.cos(angle)
                wave[index, 1] = SCALE * jnp.sin(angle)
                step = rows[7:8] * (8.0 / RANGE)
                rates[index, 0:1] = jnp.cos(step)
                rates[index, 1:2] = jnp.sin(step)
                rates[index, 2:3] = jnp.abs(rows[5:6])
                rates[index, 3:4] = rows[5:6]
            return carry

        lax.fori_loop(0, 8, prepare, 0)

    live = counts[0, 0]
    for k in range(8):
        wide[0, :, k * 256 : k * 256 + 256] = matrices[k] * jnp.where(k < live, 1.0, 0.0).astype(BF16)

    mat_copy.wait_recv()

    def maty_copy(step):
        own = pl.ds(2 * y, 2)
        return remote(other_mat.at[own], other_mat.at[own], maty_send.at[step], maty_recv.at[step], y_peer(step))

    def maty_wait(step):
        there = pl.ds(2 * ((y + 4 - step) % 4), 2)
        remote(other_mat.at[there], other_mat.at[there], maty_send.at[step], maty_recv.at[step], y_peer(step)).wait_recv()

    for step in (1, 2, 3):
        maty_copy(step).start()

    row8 = lax.broadcasted_iota(jnp.int32, (8, 128), 0)

    def run_level(level, sub):
        source, target = split.at[level % 2], split.at[(level + 1) % 2]
        start = first + sub * ROWS
        bins = start + jnp.where(low, ROWS + row8, row8 - 8)
        inside = jnp.where((bins >= 0) & (bins < RANGE), 1.0, 0.0).astype(F32)

        def one(q, carry):
            index = (level * 8 + q) * 2
            for side in range(2):
                if level == 0:
                    slot = 2 * q + side
                else:
                    bit = 1 << (level - 1)
                    half = (q // bit) % 2
                    slot = (q - half * bit + side * bit) * 2 + half
                x = source[slot]
                w = bank[index + side]
                high, rest = w[0:128], w[128:256]
                part[side] = jnp.dot(
                    jnp.concatenate([x, x], axis=1),
                    jnp.concatenate([high, high, rest, rest], axis=0),
                    preferred_element_type=F32,
                )
            for half in range(2):
                lanes = slice(half * 128, half * 128 + 128)

                def load(side, comp, t):
                    return part[side, t * 16 + comp * 8 : t * 16 + comp * 8 + 8, lanes]

                cosine = [wave[index + s, 0, :, lanes] for s in range(2)]
                sine = [wave[index + s, 1, :, lanes] for s in range(2)]
                step_c = [jnp.broadcast_to(rates[index + s, 0:1, lanes], (8, 128)) for s in range(2)]
                step_s = [jnp.broadcast_to(rates[index + s, 1:2, lanes], (8, 128)) for s in range(2)]
                amount = [jnp.broadcast_to(rates[index + s, 2:3, lanes], (8, 128)) for s in range(2)]
                ahead = [jnp.broadcast_to(rates[index + s, 3:4, lanes], (8, 128)) > 0.0 for s in range(2)]
                back_c = [cosine[s] * step_c[s] + sine[s] * step_s[s] for s in range(2)]
                back_s = [sine[s] * step_c[s] - cosine[s] * step_s[s] for s in range(2)]
                up, down = {}, {}
                for s in range(2):
                    for comp in range(2):
                        up[s, comp, 0] = pltpu.roll(load(s, comp, 0), 7, 0)
                        down[s, comp, -1] = pltpu.roll(load(s, comp, TILES - 1), 1, 0)
                previous = None
                for t in range(TILES if level < 3 else TILES - 1):
                    if t == TILES - 1:
                        if sub + 1 < SUBS:
                            for s in range(2):
                                wave[index + s, 0, :, lanes] = cosine[s]
                                wave[index + s, 1, :, lanes] = sine[s]
                        for s in range(2):
                            cosine[s] = jnp.where(low, cosine[s], back_c[s])
                            sine[s] = jnp.where(low, sine[s], back_s[s])
                    total = [None, None]
                    for s in range(2):
                        moved = []
                        for comp in range(2):
                            center = load(s, comp, t)
                            if t + 1 < TILES:
                                up[s, comp, t + 1] = pltpu.roll(load(s, comp, t + 1), 7, 0)
                                following = up[s, comp, t + 1]
                            else:
                                following = pltpu.roll(load(s, comp, 0), 7, 0)
                            down[s, comp, t] = pltpu.roll(center, 1, 0)
                            after = jnp.where(row8 == 7, following, up[s, comp, t])
                            before = jnp.where(row8 == 0, down[s, comp, t - 1], down[s, comp, t])
                            beside = jnp.where(ahead[s], after, before)
                            moved.append(center + amount[s] * (beside - center))
                        real = moved[0] * cosine[s] - moved[1] * sine[s]
                        imag = moved[0] * sine[s] + moved[1] * cosine[s]
                        total = [real, imag] if s == 0 else [total[0] + real, total[1] + imag]
                        if t < TILES - 1:
                            cosine[s], sine[s] = (
                                cosine[s] * step_c[s] - sine[s] * step_s[s],
                                sine[s] * step_c[s] + cosine[s] * step_s[s],
                            )
                    if level < 3:
                        if t == TILES - 1:
                            total = [v * inside for v in total]
                        both = jnp.concatenate(total, axis=0)
                        high = both.astype(BF16)
                        target[q * 2 + half, t * 16 : t * 16 + 16, 0:128] = high
                        target[q * 2 + half, t * 16 : t * 16 + 16, 128:256] = (both - high.astype(F32)).astype(BF16)
                    elif t % 2 == 0:
                        previous = total
                    else:
                        for comp in range(2):
                            row = comp * ROWS + (t // 2) * 16
                            gathered[0][sub][core * 8 + q, row : row + 16, lanes] = jnp.concatenate(
                                [previous[comp], total[comp]], axis=0
                            ).astype(BF16)
                if level == 3 and sub + 1 < SUBS:
                    for s in range(2):
                        wave[index + s, 0, :, lanes] = cosine[s]
                        wave[index + s, 1, :, lanes] = sine[s]
            return carry

        lax.fori_loop(0, 8, one, 0)

    own_half = pl.ds(core * 8, 8)
    pending = []

    def start(copy):
        copy.start()
        pending.append(copy)

    def core_copy(place, sub):
        ref = gathered[place][sub].at[own_half]
        n = place * 2 + sub
        return remote(ref, ref, core_send.at[n], core_recv.at[n], sibling)

    def core_wait(place, sub):
        ref = gathered[place][sub].at[pl.ds((1 - core) * 8, 8)]
        n = place * 2 + sub
        remote(ref, ref, core_send.at[n], core_recv.at[n], sibling).wait_recv()

    def ring_copy(way, sub):
        n = way * 2 + sub
        return remote(
            gathered[0][sub].at[own_half], gathered[1 + way][sub].at[own_half],
            ring_send.at[n], ring_recv.at[n], (z_next, z_prev)[way],
        )

    def relay_copy(way, sub):
        n = way * 2 + sub
        quarter = pl.ds(core * 8 + way * 4, 4)
        return remote(
            gathered[1 + way][sub].at[quarter], gathered[3][sub].at[quarter],
            relay_send.at[n], relay_recv.at[n], (z_next, z_prev)[way],
        )

    for sub in range(SUBS):

        def wait_child(step, carry, sub=sub):
            child_copy(sub, step, (a + step) % 16).wait_recv()
            return carry

        lax.fori_loop(1, 16, wait_child, 0)
        pltpu.make_async_copy(staged.at[me * 2 + sub, core], received.at[sub, a], local_sem.at[sub]).wait()

        def halve(n, carry, sub=sub):
            x = received[sub, n].reshape(TILES * 16, 128)
            high = x.astype(BF16)
            split[0, n, :, 0:128] = high
            split[0, n, :, 128:256] = (x - high.astype(F32)).astype(BF16)
            return carry

        lax.fori_loop(0, 16, halve, 0)
        for level in range(4):
            run_level(level, sub)
        for way in range(2):
            start(ring_copy(way, sub))
        start(core_copy(0, sub))

    def relay(sub):
        for way in range(2):
            ring_copy(way, sub).wait_recv()
            start(relay_copy(way, sub))
            start(core_copy(1 + way, sub))

    def far(sub):
        for way in range(2):
            relay_copy(way, sub).wait_recv()
        start(core_copy(3, sub))

    def tile_copy(n):
        return remote(sent_tiles.at[n], got_tiles.at[n], tile_send.at[n], tile_recv.at[n], x_pair)

    lane = lax.broadcasted_iota(jnp.int32, (512, 128), 1)

    def place_tile(early, late, side, place):
        where = (side * 4 + (z + (0, 3, 1, 2)[place]) % 4) * 128
        lanes = pl.ds(pl.multiple_of(where, 128), 128)
        out[0, :, lanes] = jnp.where(lane < 64, early, pltpu.roll(late, 64, 1))
        out[1, :, lanes] = jnp.where(lane < 64, pltpu.roll(early, 64, 1), late)

    def product(place, sub):
        core_wait(place, sub)
        n = place * 2 + sub
        for tile in (1, 0):
            for k in range(8):
                block = info_s[0, k] if tile else sources[0, k]
                columns[:, k * 256 : k * 256 + 256] = gathered[place][sub][(block % 2) * 8 + block // 2]
            result = lax.dot_general(
                wide[tile], columns[...], (((1,), (1,)), ((), ())), preferred_element_type=F32
            )
            if tile:
                sent_tiles[n] = result.astype(BF16)
                start(tile_copy(n))
            elif sub == 0:
                held[place] = result
            else:
                place_tile(held[place], result, xh, place)

    relay(0)
    info_copy.wait()
    listed = pltpu.make_async_copy(info_got, info_s, local_sem.at[2])
    listed.start()
    listed.wait()
    for step in (1, 2, 3):
        maty_wait(step)
    other_live = info_s[1, 0]
    for k in range(8):
        wide[1, :, k * 256 : k * 256 + 256] = other_mat[k] * jnp.where(k < other_live, 1.0, 0.0).astype(BF16)
    product(0, 0)
    product(0, 1)
    relay(1)
    product(1, 0)
    product(2, 0)
    far(0)
    product(1, 1)
    product(2, 1)
    far(1)
    product(3, 0)
    product(3, 1)
    for place in range(4):
        for sub in range(SUBS):
            tile_copy(place * 2 + sub).wait_recv()
        place_tile(got_tiles[place * 2].astype(F32), got_tiles[place * 2 + 1].astype(F32), 1 - xh, place)

    for copy in pending:
        copy.wait_send()
    for step in (1, 2, 3):
        pary_copy(step).wait_send()
        maty_copy(step).wait_send()
    mat_copy.wait_send()

    def wait_sent(step, carry):
        for sub in range(SUBS):
            child_copy(sub, step, a).wait_send()
        return carry

    lax.fori_loop(1, 16, wait_sent, 0)

    def wait_par_sent(step, carry):
        par_copy(step, me).wait_send()
        return carry

    lax.fori_loop(1, 8, wait_par_sent, 0)


def shards(child, taps, bands, shifts, bases, slopes, sources, counts, matrices):
    counts = counts.reshape(1, 1)
    matrices = matrices[0]
    vmem = pl.BlockSpec(memory_space=pltpu.VMEM)
    smem = pl.BlockSpec(memory_space=pltpu.SMEM)
    dma = pltpu.SemaphoreType.DMA
    scratch = [
        pltpu.VMEM((16, 2, TILES, 2, 8, 128), F32),
        pltpu.VMEM((2, 2, 2, 8, 128), F32),
        pltpu.VMEM((SUBS, 16, TILES, 2, 8, 128), F32),
        pltpu.VMEM((2, 16, TILES * 16, 256), BF16),
        pltpu.VMEM((2, TILES * 16, 256), F32),
        pltpu.VMEM((64, 256, 256), BF16),
        pltpu.VMEM((64, 2, 8, 256), F32),
        pltpu.VMEM((64, 8, 256), F32),
        pltpu.VMEM((4, 16, 256), F32),
        pltpu.VMEM((4, 8, 16, 256), F32),
        *[pltpu.VMEM((16, 128, 256), BF16) for _ in range(8)],
        pltpu.VMEM((8, 512, 256), BF16),
        pltpu.VMEM((2, 512, 2048), BF16),
        pltpu.VMEM((128, 2048), BF16),
        pltpu.VMEM((8, 512, 128), BF16),
        pltpu.VMEM((8, 512, 128), BF16),
        pltpu.VMEM((4, 512, 128), F32),
        pltpu.VMEM((8, 128), jnp.int32),
        pltpu.VMEM((8, 128), jnp.int32),
        pltpu.SMEM((8, 128), jnp.int32),
        dma((2, 16)), dma((2, 16)),
        dma((2,)), dma((2,)),
        dma((8,)), dma((8,)),
        dma((4,)), dma((4,)),
        dma((1,)), dma((1,)),
        dma((4,)), dma((4,)),
        dma((4,)), dma((4,)),
        dma((4,)), dma((4,)),
        dma((8,)), dma((8,)),
        dma((8,)), dma((8,)),
        dma((1,)), dma((1,)),
        dma((3,)),
    ]
    return pl.pallas_call(
        kernel,
        out_shape=jax.ShapeDtypeStruct((2, 512, 1024), F32),
        in_specs=[vmem] * 9 + [smem] * 2,
        out_specs=vmem,
        scratch_shapes=scratch,
        compiler_params=pltpu.CompilerParams(
            collective_id=0, has_side_effects=True, vmem_limit_bytes=62 * 2**20
        ),
    )(child, taps, bands, shifts, bases, slopes, sources, counts, matrices, sources, counts)


def solution(mesh):
    placed = (
        P(None, "aperture", "range"),
        P(None, None, None, "aperture"),
        P(None, None, "aperture"),
        P(None, None, "aperture"),
        P(None, None, "aperture"),
        P(None, None, "aperture"),
        P("aperture", None),
        P("aperture"),
        P("aperture", None, None, None),
    )
    return jax.shard_map(
        shards, mesh=mesh, in_specs=placed, out_specs=P(None, "aperture", "range"), check_vma=False
    )
```

time: 852 us -> 117 us (0.14)
  waiting for transfers between devices: 292 us -> 0 us
  local copies, waits for them, and re-layouts: 255 us -> 4.79 us
  other arithmetic: 189 us -> 0 us
  Pallas kernels: 0 us -> 112 us
  matrix products: 42.7 us -> 0 us
  starting transfers between devices: 29 us -> 0 us
  loops' own time: 23.9 us -> 0 us
  between operations: 14.3 us -> 0.66 us
    ppermute x12 -> x0, waiting for transfers between devices: 168 us -> none  [the longest x4 132 us: from_partner(): return lax.ppermute(value, axis, pairs)]
    gather x8 -> x0, local copies, waits for them, and re-layouts: 155 us -> none  [beam_interp(): picked = child_rows[:, row_index, :]]
    all_gather x1 -> x0, waiting for transfers between devices: 124 us -> none  [shards(): gathered_piece = lax.all_gather(polar_image, 'aperture', axis=1, tiled=True)]
    pallas_call x0 -> x1, Pallas kernels: none -> 112 us  [shards(): pl.pallas_call(kernel, out_shape=jax.ShapeDtypeStruct((2, 512, 1024), F32...]
    reduce_sum x7 -> x0, other arithmetic: 78.7 us -> none  [beam_interp(): return jnp.sum(picked * weights[None, :, :, None], axis=1)]
    sub x4 -> x0, other arithmetic: 43.3 us -> none  [finish_side(): real_part = shifted[0] * cosine - shifted[1] * sine_part]
    dot_general x8 -> x0, matrix products: 42.7 us -> none  [product(): jnp.einsum('cb,xbr->xcr', matrix, block_image, preferred_element_type=jnp...]
    concatenate x8 -> x0, local copies, waits for them, and re-layouts: 29.9 us -> none  [with_halo(): jnp.concatenate([lax.ppermute(tail, axis, [(i, (i + 1) % count) for i in...]
  transfers between devices with their start and end apart: 13 -> 0, of which waited for: 13 -> 0; matrix products, arithmetic and copies ran while one was open for 0% -> 0% of each run, Pallas kernels for 0% -> 0%
where the time goes in v1:
time: 117 us
  Pallas kernels  112 us (96%)
  local copies, waits for them, and re-layouts  4.79 us (4%)
    pallas_call x1, Pallas kernels, shards(): pl.pallas_call(kernel, out_shape=jax.ShapeDtypeStruct((2, 512, 1024), F32...  112 us
    unnamed x1, local copies, waits for them, and re-layouts  4.79 us

profile of v1, /device:TPU:1, one launch (start us, length us, event | category | flops | bytes accessed | tf_op | source)
XLA Modules:
  0.0 117.2 jit_solution(9854468972393290479)
XLA Ops:
  0.7 111.8 %shard_map.91 = f32[2,512,1024]{2,1,0:T(8,128)} custom-call(f32[2,256,1024]{2,1,0:T(8,128)} %child.1, f32[4,2,4,256]{3,2,1,0:T(4,128)} %taps.1, s32[4,2,256]{2,1,0:T(2,128)} %bands.1, f32[4,2,256]{2,1,0:T(2,128)} %shifts.1, f32[4,2,256]{2,1,0:T(2,128)} %bases.1, f32[4,2,256]{2,1,0:T(2,128)} %slopes.1, s32[1,8]{1,0:T(1,128)} %sources.1, ...), custom_call_target="tpu_custom_call" | custom-call | tf_op jit(solution)/shard_map/pallas_call | solution.py:493
  112.4 4.8 %copy.12 = f32[2,512,1024]{2,1,0:T(8,128)} copy(f32[2,512,1024]{2,1,0:T(8,128)} %shard_map.91) | data formatting | bytes 8388608

commit v2 on v1

--- a/solution.py
+++ b/solution.py
@@ -2,6 +2,7 @@
 
 import jax
 import jax.numpy as jnp
+import numpy as np
 from jax import lax
 from jax.experimental import pallas as pl
 from jax.experimental.pallas import tpu as pltpu
@@ -17,10 +18,26 @@
 BF16 = jnp.bfloat16
 
 
+def turn_by(angle):
+    quarters = jnp.round(angle * (2.0 / np.pi))
+    x = angle - quarters * 1.5703125
+    x = x - quarters * 4.838267948966e-4
+    x2 = x * x
+    sine = x + x * x2 * (-1.6666654611e-1 + x2 * (8.3321608736e-3 - x2 * 1.9515295891e-4))
+    cosine = 1.0 - 0.5 * x2 + x2 * x2 * (4.166664568298827e-2 + x2 * (-1.388731625493765e-3 + x2 * 2.443315711809948e-5))
+    part = quarters - 4.0 * jnp.floor(quarters * 0.25)
+    odd = (part == 1.0) | (part == 3.0)
+    first = jnp.where(odd, sine, cosine)
+    second = jnp.where(odd, cosine, sine)
+    first = jnp.where((part == 1.0) | (part == 2.0), -first, first)
+    second = jnp.where(part >= 2.0, -second, second)
+    return first, second
+
+
 def kernel(
-    child, taps, bands, shifts, bases, slopes, sources_v, counts_v, matrices, sources, counts,
+    child_h, taps, bands, shifts, bases, slopes, sources_v, counts_v, matrices, sources, counts,
     out,
-    staged, edges, received, split, part, bank, wave, rates, own_par, par,
+    child, own_mat, staged, edges, coded, received, split, part, bank, wave, rates, own_par, par,
     g00, g01, g10, g11, g20, g21, g30, g31,
     other_mat, wide, columns, sent_tiles, got_tiles, held, info, info_got, info_s,
     a2a_send, a2a_recv, edge_send, edge_recv, par_send, par_recv, pary_send, pary_recv,
@@ -44,6 +61,11 @@
     def y_peer(step):
         return (a, ((y + step) % 4) * 2 + xl)
 
+    load_child = pltpu.make_async_copy(child_h, child, local_sem.at[3])
+    load_child.start()
+    load_mat = pltpu.make_async_copy(matrices, own_mat, local_sem.at[4])
+    load_mat.start()
+
     barrier = pltpu.get_barrier_semaphore()
 
     def greet(step, carry):
@@ -66,29 +88,7 @@
     info[0:1, 0:8] = sources_v[...]
     info[1:2, 0:1] = counts_v[...]
 
-    pl.semaphore_wait(barrier, 21)
-
-    def remote(src, dst, send, recv, to):
-        return pltpu.make_async_remote_copy(
-            src_ref=src, dst_ref=dst, send_sem=send, recv_sem=recv, device_id=to, device_id_type=MESH
-        )
-
-    def par_copy(step, slot):
-        return remote(
-            own_par.at[y], par.at[y, slot], par_send.at[step], par_recv.at[slot], ((a + 2 * step) % 16, p)
-        )
-
-    def send_par(step, carry):
-        par_copy(step, me).start()
-        return carry
-
-    lax.fori_loop(1, 8, send_par, 0)
-    mat_copy = remote(
-        matrices.at[pl.ds(2 * y, 2)], other_mat.at[pl.ds(2 * y, 2)], mat_send.at[0], mat_recv.at[0], x_side
-    )
-    mat_copy.start()
-    info_copy = remote(info, info_got, info_send.at[0], info_recv.at[0], x_pair)
-    info_copy.start()
+    load_child.wait()
 
     def turn(k, carry):
         for comp in range(2):
@@ -100,6 +100,41 @@
         return carry
 
     lax.fori_loop(0, 8, turn, 0)
+
+    pl.semaphore_wait(barrier, 21)
+
+    def remote(src, dst, send, recv, to):
+        return pltpu.make_async_remote_copy(
+            src_ref=src, dst_ref=dst, send_sem=send, recv_sem=recv, device_id=to, device_id_type=MESH
+        )
+
+    there = p + 1 - 2 * (p % 2)
+
+    def mat_first(n):
+        return remote(
+            matrices.at[pl.ds(n, 1)], other_mat.at[pl.ds(n, 1)], mat_send.at[0], mat_recv.at[0], x_side
+        )
+
+    def mat_second(n):
+        return remote(
+            other_mat.at[pl.ds(n, 1)], other_mat.at[pl.ds(n, 1)], mat_send.at[1], mat_recv.at[1], (a, there)
+        )
+
+    mat_first(p).start()
+
+    def par_copy(step, slot):
+        return remote(
+            own_par.at[y], par.at[y, slot], par_send.at[step], par_recv.at[slot], ((a + 2 * step) % 16, p)
+        )
+
+    def send_par(step, carry):
+        par_copy(step, me).start()
+        return carry
+
+    lax.fori_loop(1, 8, send_par, 0)
+    info_copy = remote(info, info_got, info_send.at[0], info_recv.at[0], x_pair)
+    info_copy.start()
+
     edge_next = remote(staged.at[15, :, 7], edges.at[0], edge_send.at[0], edge_recv.at[0], r_next)
     edge_prev = remote(staged.at[0, :, 0], edges.at[1], edge_send.at[1], edge_recv.at[1], r_prev)
     edge_next.start()
@@ -112,7 +147,49 @@
                 staged[j, half, 8, comp] = jnp.where(low, staged[j + 1, half, 0, comp], staged[j - 1, half, 7, comp])
         return carry
 
-    lax.fori_loop(1, 15, fill, 0)
+    def code(j, carry):
+        for half in range(2):
+            x = staged[j, half].reshape(TILES * 16, 128)
+            most = jnp.max(jnp.abs(x), axis=0, keepdims=True)
+            power = jnp.ceil(jnp.log2(jnp.maximum(most, 1e-30)) - 14.9999)
+            coded[j, half, 0 : TILES * 16] = jnp.round(x * jnp.exp2(-power)).astype(jnp.int16)
+            coded[j, half, TILES * 16 : TILES * 16 + 16] = jnp.broadcast_to(power, (16, 128)).astype(jnp.int16)
+        return carry
+
+    def fill_code(j, carry):
+        return code(j, fill(j, carry))
+
+    def child_copy(sub, step, slot):
+        to = (a + step) % 16
+        return remote(
+            coded.at[(to // 2) * 2 + sub, to % 2],
+            received.at[sub, slot],
+            a2a_send.at[sub, step],
+            a2a_recv.at[sub, slot],
+            (to, p),
+        )
+
+    def keep_copy(sub):
+        return pltpu.make_async_copy(coded.at[me * 2 + sub, core], received.at[sub, a], local_sem.at[sub])
+
+    def send_children(sub, edge):
+        last = 7 * sub
+
+        def send_child(step, carry):
+            @pl.when((((a + step) % 16) // 2 == last) == edge)
+            def _():
+                child_copy(sub, step, a).start()
+
+            return carry
+
+        lax.fori_loop(1, 16, send_child, 0)
+
+        @pl.when((me == last) == edge)
+        def _():
+            keep_copy(sub).start()
+
+    lax.fori_loop(1, 15, fill_code, 0)
+    send_children(0, False)
     edge_next.wait()
     edge_prev.wait()
     has_prev = jnp.where(p > 0, 1.0, 0.0).astype(F32)
@@ -121,25 +198,9 @@
         for comp in range(2):
             staged[0, half, 8, comp] = jnp.where(low, staged[1, half, 0, comp], edges[0, half, comp] * has_prev)
             staged[15, half, 8, comp] = jnp.where(low, edges[1, half, comp] * has_next, staged[14, half, 7, comp])
-
-    def child_copy(sub, step, slot):
-        to = (a + step) % 16
-        return remote(
-            staged.at[(to // 2) * 2 + sub, to % 2],
-            received.at[sub, slot],
-            a2a_send.at[sub, step],
-            a2a_recv.at[sub, slot],
-            (to, p),
-        )
-
-    for sub in range(SUBS):
-
-        def send_child(step, carry, sub=sub):
-            child_copy(sub, step, a).start()
-            return carry
-
-        lax.fori_loop(1, 16, send_child, 0)
-        pltpu.make_async_copy(staged.at[me * 2 + sub, core], received.at[sub, a], local_sem.at[sub]).start()
+    code(0, 0)
+    code(15, 0)
+    send_children(0, True)
 
     par[y, me] = own_par[y]
 
@@ -158,11 +219,43 @@
 
     for step in (1, 2, 3):
         pary_copy(step).start()
+
+    def maty_copy(piece, step):
+        own = pl.ds((there, p)[piece], 1)
+        n = piece * 4 + step
+        return remote(other_mat.at[own], other_mat.at[own], maty_send.at[n], maty_recv.at[n], y_peer(step))
+
+    def maty_wait(piece, step):
+        p_far = ((y + 4 - step) % 4) * 2 + xl
+        far = pl.ds((p_far + 1 - 2 * (p_far % 2), p_far)[piece], 1)
+        n = piece * 4 + step
+        remote(other_mat.at[far], other_mat.at[far], maty_send.at[n], maty_recv.at[n], y_peer(step)).wait_recv()
+
+    mat_first(there).wait_recv()
+    for step in (1, 3, 2):
+        maty_copy(0, step).start()
+    mat_second(there).start()
+
+    load_mat.wait()
+    live = counts[0, 0]
+    for k in range(8):
+        wide[0, :, k * 256 : k * 256 + 256] = own_mat[k] * jnp.where(k < live, 1.0, 0.0).astype(BF16)
+
+    def wait_sent(step, carry):
+        child_copy(0, step, a).wait_send()
+        return carry
+
+    lax.fori_loop(1, 16, wait_sent, 0)
+    send_children(1, False)
+    send_children(1, True)
     for step in (1, 2, 3):
         pary_wait(step)
+    mat_second(p).wait_recv()
+    for step in (1, 3, 2):
+        maty_copy(1, step).start()
 
     first = p * 1024 + me * (SUBS * ROWS)
-    beam = lax.broadcasted_iota(jnp.int32, (128, 256), 0).astype(F32)
+    beam = lax.broadcasted_iota(jnp.int32, (128, 256), 0).astype(F32).astype(BF16)
     radius = (first + lax.broadcasted_iota(jnp.int32, (8, 256), 0)).astype(F32) * (1.0 / RANGE)
     for level in range(4):
 
@@ -172,41 +265,30 @@
             for side in range(2):
                 index = (level * 8 + q) * 2 + side
                 rows = par[level, q, side * 8 : side * 8 + 8, :]
-                offset = beam - (rows[4:5] - start)
-                banded = jnp.zeros((128, 256), F32)
+                place = rows[4:5] - start
+                weight = rows[0:4]
+                high = weight.astype(BF16)
+                rest = (weight - high.astype(F32)).astype(BF16)
+                tops = jnp.zeros((128, 256), BF16)
+                tails = jnp.zeros((128, 256), BF16)
                 for tap in range(4):
-                    banded = jnp.where(offset == float(tap), rows[tap : tap + 1], banded)
-                high = banded.astype(BF16)
-                bank[index, 0:128] = high
-                bank[index, 128:256] = (banded - high.astype(F32)).astype(BF16)
-                angle = rows[6:7] + rows[7:8] * radius
-                wave[index, 0] = SCALE * jnp.cos(angle)
-                wave[index, 1] = SCALE * jnp.sin(angle)
+                    hit = beam == (place + float(tap)).astype(BF16)
+                    tops = jnp.where(hit, high[tap : tap + 1], tops)
+                    tails = jnp.where(hit, rest[tap : tap + 1], tails)
+                bank[index, 0:128] = tops
+                bank[index, 128:256] = tails
+                cosine, sine = turn_by(rows[6:7] + rows[7:8] * radius)
+                wave[index, 0] = SCALE * cosine
+                wave[index, 1] = SCALE * sine
                 step = rows[7:8] * (8.0 / RANGE)
-                rates[index, 0:1] = jnp.cos(step)
-                rates[index, 1:2] = jnp.sin(step)
+                step2 = step * step
+                rates[index, 0:1] = 1.0 - 0.5 * step2 + step2 * step2 * (1.0 / 24.0)
+                rates[index, 1:2] = step - step * step2 * (1.0 / 6.0)
                 rates[index, 2:3] = jnp.abs(rows[5:6])
                 rates[index, 3:4] = rows[5:6]
             return carry
 
         lax.fori_loop(0, 8, prepare, 0)
-
-    live = counts[0, 0]
-    for k in range(8):
-        wide[0, :, k * 256 : k * 256 + 256] = matrices[k] * jnp.where(k < live, 1.0, 0.0).astype(BF16)
-
-    mat_copy.wait_recv()
-
-    def maty_copy(step):
-        own = pl.ds(2 * y, 2)
-        return remote(other_mat.at[own], other_mat.at[own], maty_send.at[step], maty_recv.at[step], y_peer(step))
-
-    def maty_wait(step):
-        there = pl.ds(2 * ((y + 4 - step) % 4), 2)
-        remote(other_mat.at[there], other_mat.at[there], maty_send.at[step], maty_recv.at[step], y_peer(step)).wait_recv()
-
-    for step in (1, 2, 3):
-        maty_copy(step).start()
 
     row8 = lax.broadcasted_iota(jnp.int32, (8, 128), 0)
 
@@ -347,10 +429,11 @@
             return carry
 
         lax.fori_loop(1, 16, wait_child, 0)
-        pltpu.make_async_copy(staged.at[me * 2 + sub, core], received.at[sub, a], local_sem.at[sub]).wait()
+        keep_copy(sub).wait()
 
         def halve(n, carry, sub=sub):
-            x = received[sub, n].reshape(TILES * 16, 128)
+            power = received[sub, n, TILES * 16 : TILES * 16 + 16].astype(F32)[0:1]
+            x = received[sub, n, 0 : TILES * 16].astype(F32) * jnp.exp2(power)
             high = x.astype(BF16)
             split[0, n, :, 0:128] = high
             split[0, n, :, 128:256] = (x - high.astype(F32)).astype(BF16)
@@ -385,45 +468,53 @@
         out[0, :, lanes] = jnp.where(lane < 64, early, pltpu.roll(late, 64, 1))
         out[1, :, lanes] = jnp.where(lane < 64, pltpu.roll(early, 64, 1), late)
 
-    def product(place, sub):
-        core_wait(place, sub)
+    def product(place, sub, tile):
         n = place * 2 + sub
-        for tile in (1, 0):
-            for k in range(8):
-                block = info_s[0, k] if tile else sources[0, k]
-                columns[:, k * 256 : k * 256 + 256] = gathered[place][sub][(block % 2) * 8 + block // 2]
-            result = lax.dot_general(
-                wide[tile], columns[...], (((1,), (1,)), ((), ())), preferred_element_type=F32
-            )
-            if tile:
-                sent_tiles[n] = result.astype(BF16)
-                start(tile_copy(n))
-            elif sub == 0:
-                held[place] = result
-            else:
-                place_tile(held[place], result, xh, place)
-
+        for k in range(8):
+            block = info_s[0, k] if tile else sources[0, k]
+            columns[:, k * 256 : k * 256 + 256] = gathered[place][sub][(block % 2) * 8 + block // 2]
+        result = lax.dot_general(
+            wide[tile], columns[...], (((1,), (1,)), ((), ())), preferred_element_type=F32
+        )
+        if tile:
+            sent_tiles[n] = result.astype(BF16)
+            start(tile_copy(n))
+        elif sub == 0:
+            held[place] = result
+        else:
+            place_tile(held[place], result, xh, place)
+
+    for sub in range(SUBS):
+        core_wait(0, sub)
+        product(0, sub, 0)
     relay(0)
     info_copy.wait()
     listed = pltpu.make_async_copy(info_got, info_s, local_sem.at[2])
     listed.start()
     listed.wait()
-    for step in (1, 2, 3):
-        maty_wait(step)
+    for piece in range(2):
+        for step in (1, 2, 3):
+            maty_wait(piece, step)
     other_live = info_s[1, 0]
     for k in range(8):
         wide[1, :, k * 256 : k * 256 + 256] = other_mat[k] * jnp.where(k < other_live, 1.0, 0.0).astype(BF16)
-    product(0, 0)
-    product(0, 1)
+    product(0, 0, 1)
+    product(0, 1, 1)
+
+    def both(place, sub):
+        core_wait(place, sub)
+        product(place, sub, 1)
+        product(place, sub, 0)
+
+    both(1, 0)
+    both(2, 0)
     relay(1)
-    product(1, 0)
-    product(2, 0)
     far(0)
-    product(1, 1)
-    product(2, 1)
+    both(1, 1)
+    both(2, 1)
     far(1)
-    product(3, 0)
-    product(3, 1)
+    both(3, 0)
+    both(3, 1)
     for place in range(4):
         for sub in range(SUBS):
             tile_copy(place * 2 + sub).wait_recv()
@@ -433,15 +524,16 @@
         copy.wait_send()
     for step in (1, 2, 3):
         pary_copy(step).wait_send()
-        maty_copy(step).wait_send()
-    mat_copy.wait_send()
-
-    def wait_sent(step, carry):
-        for sub in range(SUBS):
-            child_copy(sub, step, a).wait_send()
-        return carry
-
-    lax.fori_loop(1, 16, wait_sent, 0)
+        for piece in range(2):
+            maty_copy(piece, step).wait_send()
+    mat_first(p).wait_send()
+    mat_second(there).wait_send()
+
+    def wait_last_sent(step, carry):
+        child_copy(1, step, a).wait_send()
+        return carry
+
+    lax.fori_loop(1, 16, wait_last_sent, 0)
 
     def wait_par_sent(step, carry):
         par_copy(step, me).wait_send()
@@ -455,11 +547,15 @@
     matrices = matrices[0]
     vmem = pl.BlockSpec(memory_space=pltpu.VMEM)
     smem = pl.BlockSpec(memory_space=pltpu.SMEM)
+    hbm = pl.BlockSpec(memory_space=pl.ANY)
     dma = pltpu.SemaphoreType.DMA
     scratch = [
+        pltpu.VMEM((2, 256, 1024), F32),
+        pltpu.VMEM((8, 512, 256), BF16),
         pltpu.VMEM((16, 2, TILES, 2, 8, 128), F32),
         pltpu.VMEM((2, 2, 2, 8, 128), F32),
-        pltpu.VMEM((SUBS, 16, TILES, 2, 8, 128), F32),
+        pltpu.VMEM((16, 2, TILES * 16 + 16, 128), jnp.int16),
+        pltpu.VMEM((SUBS, 16, TILES * 16 + 16, 128), jnp.int16),
         pltpu.VMEM((2, 16, TILES * 16, 256), BF16),
         pltpu.VMEM((2, TILES * 16, 256), F32),
         pltpu.VMEM((64, 256, 256), BF16),
@@ -481,23 +577,23 @@
         dma((2,)), dma((2,)),
         dma((8,)), dma((8,)),
         dma((4,)), dma((4,)),
-        dma((1,)), dma((1,)),
-        dma((4,)), dma((4,)),
+        dma((2,)), dma((2,)),
+        dma((8,)), dma((8,)),
         dma((4,)), dma((4,)),
         dma((4,)), dma((4,)),
         dma((8,)), dma((8,)),
         dma((8,)), dma((8,)),
         dma((1,)), dma((1,)),
-        dma((3,)),
+        dma((5,)),
     ]
     return pl.pallas_call(
         kernel,
-        out_shape=jax.ShapeDtypeStruct((2, 512, 1024), F32),
-        in_specs=[vmem] * 9 + [smem] * 2,
+        out_shape=pltpu.VMEM((2, 512, 1024), F32),
+        in_specs=[hbm] + [vmem] * 7 + [hbm] + [smem] * 2,
         out_specs=vmem,
         scratch_shapes=scratch,
         compiler_params=pltpu.CompilerParams(
-            collective_id=0, has_side_effects=True, vmem_limit_bytes=62 * 2**20
+            collective_id=0, has_side_effects=True, vmem_limit_bytes=56 * 2**20
         ),
     )(child, taps, bands, shifts, bases, slopes, sources, counts, matrices, sources, counts)
 

time: 117 us -> 101 us (0.86)
  Pallas kernels: 112 us -> 97.9 us
  local copies, waits for them, and re-layouts: 4.79 us -> 2.02 us
    pallas_call x1, Pallas kernels: 112 us -> 97.9 us  [shards(): pl.pallas_call(kernel, out_shape=pltpu.VMEM((2, 512, 1024), F32), in_spec...]
    unnamed x1, local copies, waits for them, and re-layouts: 4.79 us -> 2.02 us
where the time goes in v2:
time: 101 us
  Pallas kernels  97.9 us (97%)
  local copies, waits for them, and re-layouts  2.02 us (2%)
    pallas_call x1, Pallas kernels, shards(): pl.pallas_call(kernel, out_shape=pltpu.VMEM((2, 512, 1024), F32), in_spec...  97.9 us

profile of v2, /device:TPU:1, one launch (start us, length us, event | category | flops | bytes accessed | tf_op | source)
XLA Modules:
  0.0 100.6 jit_solution(9997179556503304623)
XLA Ops:
  0.7 97.9 %shard_map.91 = f32[2,512,1024]{2,1,0:T(8,128)S(1)} custom-call(f32[2,256,1024]{2,1,0:T(8,128)} %child_h.1, f32[4,2,4,256]{3,2,1,0:T(4,128)} %taps.1, s32[4,2,256]{2,1,0:T(2,128)} %bands.1, f32[4,2,256]{2,1,0:T(2,128)} %shifts.1, f32[4,2,256]{2,1,0:T(2,128)} %bases.1, f32[4,2,256]{2,1,0:T(2,128)} %slopes.1, s32[1,8]{1,0:T(1,128)} %sources.1, ...), custom_call_target="tpu_custom_call" | custom-call | tf_op jit(solution)/shard_map/pallas_call | solution.py:589
  98.6 2.0 %copy.11 = f32[2,512,1024]{2,1,0:T(8,128)} copy(f32[2,512,1024]{2,1,0:T(8,128)S(1)} %shard_map.91) | data formatting | bytes 8388608

commit v3 on v2

--- a/solution.py
+++ b/solution.py
@@ -37,7 +37,7 @@
 def kernel(
     child_h, taps, bands, shifts, bases, slopes, sources_v, counts_v, matrices, sources, counts,
     out,
-    child, own_mat, staged, edges, coded, received, split, part, bank, wave, rates, own_par, par,
+    child, own_mat, staged, edges, coded, received, split, part0, part1, bank, wave, rates, own_par, par,
     g00, g01, g10, g11, g20, g21, g30, g31,
     other_mat, wide, columns, sent_tiles, got_tiles, held, info, info_got, info_s,
     a2a_send, a2a_recv, edge_send, edge_recv, par_send, par_recv, pary_send, pary_recv,
@@ -110,17 +110,15 @@
 
     there = p + 1 - 2 * (p % 2)
 
-    def mat_first(n):
+    def mat_first(n, part):
+        where = other_mat.at[pl.ds(n, 1), part * 64 : part * 64 + 64]
         return remote(
-            matrices.at[pl.ds(n, 1)], other_mat.at[pl.ds(n, 1)], mat_send.at[0], mat_recv.at[0], x_side
+            matrices.at[pl.ds(n, 1), part * 64 : part * 64 + 64], where, mat_send.at[part], mat_recv.at[part], x_side
         )
 
-    def mat_second(n):
-        return remote(
-            other_mat.at[pl.ds(n, 1)], other_mat.at[pl.ds(n, 1)], mat_send.at[1], mat_recv.at[1], (a, there)
-        )
-
-    mat_first(p).start()
+    def mat_second(n, part):
+        where = other_mat.at[pl.ds(n, 1), part * 64 : part * 64 + 64]
+        return remote(where, where, mat_send.at[8 + part], mat_recv.at[8 + part], (a, there))
 
     def par_copy(step, slot):
         return remote(
@@ -134,6 +132,8 @@
     lax.fori_loop(1, 8, send_par, 0)
     info_copy = remote(info, info_got, info_send.at[0], info_recv.at[0], x_pair)
     info_copy.start()
+    for part in range(8):
+        mat_first(p, part).start()
 
     edge_next = remote(staged.at[15, :, 7], edges.at[0], edge_send.at[0], edge_recv.at[0], r_next)
     edge_prev = remote(staged.at[0, :, 0], edges.at[1], edge_send.at[1], edge_recv.at[1], r_prev)
@@ -225,16 +225,26 @@
         n = piece * 4 + step
         return remote(other_mat.at[own], other_mat.at[own], maty_send.at[n], maty_recv.at[n], y_peer(step))
 
+    def far_piece(piece, step):
+        p_far = ((y + 4 - step) % 4) * 2 + xl
+        return pl.ds((p_far + 1 - 2 * (p_far % 2), p_far)[piece], 1)
+
     def maty_wait(piece, step):
-        p_far = ((y + 4 - step) % 4) * 2 + xl
-        far = pl.ds((p_far + 1 - 2 * (p_far % 2), p_far)[piece], 1)
+        far = far_piece(piece, step)
         n = piece * 4 + step
         remote(other_mat.at[far], other_mat.at[far], maty_send.at[n], maty_recv.at[n], y_peer(step)).wait_recv()
 
-    mat_first(there).wait_recv()
-    for step in (1, 3, 2):
+    def maty_relay(piece):
+        step = (1, 3)[piece]
+        far = far_piece(piece, step)
+        n = piece * 4 + 2
+        return remote(other_mat.at[far], other_mat.at[far], maty_send.at[n], maty_recv.at[n], y_peer(step))
+
+    for part in range(8):
+        mat_first(there, part).wait_recv()
+        mat_second(there, part).start()
+    for step in (1, 3):
         maty_copy(0, step).start()
-    mat_second(there).start()
 
     load_mat.wait()
     live = counts[0, 0]
@@ -250,8 +260,9 @@
     send_children(1, True)
     for step in (1, 2, 3):
         pary_wait(step)
-    mat_second(p).wait_recv()
-    for step in (1, 3, 2):
+    for part in range(8):
+        mat_second(p, part).wait_recv()
+    for step in (3, 1):
         maty_copy(1, step).start()
 
     first = p * 1024 + me * (SUBS * ROWS)
@@ -290,6 +301,9 @@
 
         lax.fori_loop(0, 8, prepare, 0)
 
+    maty_wait(0, 1)
+    maty_relay(0).start()
+
     row8 = lax.broadcasted_iota(jnp.int32, (8, 128), 0)
 
     def run_level(level, sub):
@@ -298,7 +312,7 @@
         bins = start + jnp.where(low, ROWS + row8, row8 - 8)
         inside = jnp.where((bins >= 0) & (bins < RANGE), 1.0, 0.0).astype(F32)
 
-        def one(q, carry):
+        def multiply(q, part):
             index = (level * 8 + q) * 2
             for side in range(2):
                 if level == 0:
@@ -311,10 +325,13 @@
                 w = bank[index + side]
                 high, rest = w[0:128], w[128:256]
                 part[side] = jnp.dot(
-                    jnp.concatenate([x, x], axis=1),
-                    jnp.concatenate([high, high, rest, rest], axis=0),
+                    jnp.concatenate([x, x[:, 0:128]], axis=1),
+                    jnp.concatenate([high, high, rest], axis=0),
                     preferred_element_type=F32,
                 )
+
+        def combine(q, part):
+            index = (level * 8 + q) * 2
             for half in range(2):
                 lanes = slice(half * 128, half * 128 + 128)
 
@@ -386,9 +403,16 @@
                     for s in range(2):
                         wave[index + s, 0, :, lanes] = cosine[s]
                         wave[index + s, 1, :, lanes] = sine[s]
+
+        def two(pair, carry):
+            multiply(2 * pair + 1, part1)
+            combine(2 * pair, part0)
+            multiply((2 * pair + 2) % 8, part0)
+            combine(2 * pair + 1, part1)
             return carry
 
-        lax.fori_loop(0, 8, one, 0)
+        multiply(0, part0)
+        lax.fori_loop(0, 4, two, 0)
 
     own_half = pl.ds(core * 8, 8)
     pending = []
@@ -403,9 +427,18 @@
         return remote(ref, ref, core_send.at[n], core_recv.at[n], sibling)
 
     def core_wait(place, sub):
+        if place == 3:
+            for way in range(2):
+                core_far(way, sub, 1 - core).wait_recv()
+            return
         ref = gathered[place][sub].at[pl.ds((1 - core) * 8, 8)]
         n = place * 2 + sub
         remote(ref, ref, core_send.at[n], core_recv.at[n], sibling).wait_recv()
+
+    def core_far(way, sub, side=core):
+        ref = gathered[3][sub].at[pl.ds(side * 8 + way * 4, 4)]
+        n = 6 + sub if way == 0 else 8 + sub
+        return remote(ref, ref, core_send.at[n], core_recv.at[n], sibling)
 
     def ring_copy(way, sub):
         n = way * 2 + sub
@@ -445,6 +478,9 @@
         for way in range(2):
             start(ring_copy(way, sub))
         start(core_copy(0, sub))
+        if sub == 0:
+            maty_wait(1, 3)
+            maty_relay(1).start()
 
     def relay(sub):
         for way in range(2):
@@ -455,7 +491,7 @@
     def far(sub):
         for way in range(2):
             relay_copy(way, sub).wait_recv()
-        start(core_copy(3, sub))
+            start(core_far(way, sub))
 
     def tile_copy(n):
         return remote(sent_tiles.at[n], got_tiles.at[n], tile_send.at[n], tile_recv.at[n], x_pair)
@@ -492,9 +528,8 @@
     listed = pltpu.make_async_copy(info_got, info_s, local_sem.at[2])
     listed.start()
     listed.wait()
-    for piece in range(2):
-        for step in (1, 2, 3):
-            maty_wait(piece, step)
+    for piece, step in ((0, 3), (0, 2), (1, 1), (1, 2)):
+        maty_wait(piece, step)
     other_live = info_s[1, 0]
     for k in range(8):
         wide[1, :, k * 256 : k * 256 + 256] = other_mat[k] * jnp.where(k < other_live, 1.0, 0.0).astype(BF16)
@@ -525,9 +560,10 @@
     for step in (1, 2, 3):
         pary_copy(step).wait_send()
         for piece in range(2):
-            maty_copy(piece, step).wait_send()
-    mat_first(p).wait_send()
-    mat_second(there).wait_send()
+            (maty_relay(piece) if step == 2 else maty_copy(piece, step)).wait_send()
+    for part in range(8):
+        mat_first(p, part).wait_send()
+        mat_second(there, part).wait_send()
 
     def wait_last_sent(step, carry):
         child_copy(1, step, a).wait_send()
@@ -557,6 +593,7 @@
         pltpu.VMEM((16, 2, TILES * 16 + 16, 128), jnp.int16),
         pltpu.VMEM((SUBS, 16, TILES * 16 + 16, 128), jnp.int16),
         pltpu.VMEM((2, 16, TILES * 16, 256), BF16),
+        pltpu.VMEM((2, TILES * 16, 256), F32),
         pltpu.VMEM((2, TILES * 16, 256), F32),
         pltpu.VMEM((64, 256, 256), BF16),
         pltpu.VMEM((64, 2, 8, 256), F32),
@@ -577,11 +614,11 @@
         dma((2,)), dma((2,)),
         dma((8,)), dma((8,)),
         dma((4,)), dma((4,)),
-        dma((2,)), dma((2,)),
+        dma((16,)), dma((16,)),
         dma((8,)), dma((8,)),
         dma((4,)), dma((4,)),
         dma((4,)), dma((4,)),
-        dma((8,)), dma((8,)),
+        dma((10,)), dma((10,)),
         dma((8,)), dma((8,)),
         dma((1,)), dma((1,)),
         dma((5,)),

time: 101 us -> 91.7 us (0.908)
  Pallas kernels: 97.9 us -> 88.2 us
    pallas_call x1, Pallas kernels: 97.9 us -> 88.2 us  [shards(): pl.pallas_call(kernel, out_shape=pltpu.VMEM((2, 512, 1024), F32), in_spec...]
where the time goes in v3:
time: 91.7 us; the launch traced here: 90.8 us
  Pallas kernels  88.2 us (96%)
  local copies, waits for them, and re-layouts  2.02 us (2%)
    pallas_call x1, Pallas kernels, shards(): pl.pallas_call(kernel, out_shape=pltpu.VMEM((2, 512, 1024), F32), in_spec...  88.2 us
    unnamed x1, local copies, waits for them, and re-layouts  2.02 us

profile of v3, /device:TPU:1, one launch (start us, length us, event | category | flops | bytes accessed | tf_op | source)
XLA Modules:
  0.0 90.8 jit_solution(3318459349158315700)
XLA Ops:
  0.7 88.2 %shard_map.91 = f32[2,512,1024]{2,1,0:T(8,128)S(1)} custom-call(f32[2,256,1024]{2,1,0:T(8,128)} %child_h.1, f32[4,2,4,256]{3,2,1,0:T(4,128)} %taps.1, s32[4,2,256]{2,1,0:T(2,128)} %bands.1, f32[4,2,256]{2,1,0:T(2,128)} %shifts.1, f32[4,2,256]{2,1,0:T(2,128)} %bases.1, f32[4,2,256]{2,1,0:T(2,128)} %slopes.1, s32[1,8]{1,0:T(1,128)} %sources.1, ...), custom_call_target="tpu_custom_call" | custom-call | tf_op jit(solution)/shard_map/pallas_call | solution.py:626
  88.8 2.0 %copy.11 = f32[2,512,1024]{2,1,0:T(8,128)} copy(f32[2,512,1024]{2,1,0:T(8,128)S(1)} %shard_map.91) | data formatting | bytes 8388608

commit v4 on v3

--- a/solution.py
+++ b/solution.py
@@ -541,14 +541,22 @@
         product(place, sub, 1)
         product(place, sub, 0)
 
-    both(1, 0)
-    both(2, 0)
+    for place in (1, 2):
+        core_wait(place, 0)
+        product(place, 0, 1)
     relay(1)
+    product(1, 0, 0)
+    product(2, 0, 0)
+    for place in (1, 2):
+        core_wait(place, 1)
+        product(place, 1, 1)
     far(0)
-    both(1, 1)
-    both(2, 1)
+    core_wait(3, 0)
+    product(3, 0, 1)
+    product(1, 1, 0)
+    product(2, 1, 0)
+    product(3, 0, 0)
     far(1)
-    both(3, 0)
     both(3, 1)
     for place in range(4):
         for sub in range(SUBS):

time: 91.7 us -> 90.6 us (0.988)
  Pallas kernels: 88.2 us -> 86.3 us
    pallas_call x1, Pallas kernels: 88.2 us -> 86.3 us  [shards(): pl.pallas_call(kernel, out_shape=pltpu.VMEM((2, 512, 1024), F32), in_spec...]
where the time goes in v4:
time: 90.6 us; the launch traced here: 88.9 us
  Pallas kernels  86.3 us (95%)
  local copies, waits for them, and re-layouts  2.02 us (2%)
    pallas_call x1, Pallas kernels, shards(): pl.pallas_call(kernel, out_shape=pltpu.VMEM((2, 512, 1024), F32), in_spec...  86.3 us
    unnamed x1, local copies, waits for them, and re-layouts  2.02 us

profile of v4, /device:TPU:1, one launch (start us, length us, event | category | flops | bytes accessed | tf_op | source)
XLA Modules:
  0.0 88.9 jit_solution(17385614574071137598)
XLA Ops:
  0.7 86.3 %shard_map.91 = f32[2,512,1024]{2,1,0:T(8,128)S(1)} custom-call(f32[2,256,1024]{2,1,0:T(8,128)} %child_h.1, f32[4,2,4,256]{3,2,1,0:T(4,128)} %taps.1, s32[4,2,256]{2,1,0:T(2,128)} %bands.1, f32[4,2,256]{2,1,0:T(2,128)} %shifts.1, f32[4,2,256]{2,1,0:T(2,128)} %bases.1, f32[4,2,256]{2,1,0:T(2,128)} %slopes.1, s32[1,8]{1,0:T(1,128)} %sources.1, ...), custom_call_target="tpu_custom_call" | custom-call | tf_op jit(solution)/shard_map/pallas_call | solution.py:634
  86.9 2.0 %copy.11 = f32[2,512,1024]{2,1,0:T(8,128)} copy(f32[2,512,1024]{2,1,0:T(8,128)S(1)} %shard_map.91) | data formatting | bytes 8388608

commit v5 on v4

--- a/solution.py
+++ b/solution.py
@@ -245,11 +245,6 @@
         mat_second(there, part).start()
     for step in (1, 3):
         maty_copy(0, step).start()
-
-    load_mat.wait()
-    live = counts[0, 0]
-    for k in range(8):
-        wide[0, :, k * 256 : k * 256 + 256] = own_mat[k] * jnp.where(k < live, 1.0, 0.0).astype(BF16)
 
     def wait_sent(step, carry):
         child_copy(0, step, a).wait_send()
@@ -440,11 +435,12 @@
         n = 6 + sub if way == 0 else 8 + sub
         return remote(ref, ref, core_send.at[n], core_recv.at[n], sibling)
 
-    def ring_copy(way, sub):
+    def ring_copy(way, sub, part):
         n = way * 2 + sub
+        piece = pl.ds(core * 8 + part * 4, 4)
         return remote(
-            gathered[0][sub].at[own_half], gathered[1 + way][sub].at[own_half],
-            ring_send.at[n], ring_recv.at[n], (z_next, z_prev)[way],
+            gathered[0][sub].at[piece], gathered[1 + way][sub].at[piece],
+            ring_send.at[n, part], ring_recv.at[n, part], (z_next, z_prev)[way],
         )
 
     def relay_copy(way, sub):
@@ -475,17 +471,20 @@
         lax.fori_loop(0, 16, halve, 0)
         for level in range(4):
             run_level(level, sub)
+            if sub == 0 and level == 1:
+                maty_wait(1, 3)
+                maty_relay(1).start()
         for way in range(2):
-            start(ring_copy(way, sub))
+            for part in (way, 1 - way):
+                start(ring_copy(way, sub, part))
         start(core_copy(0, sub))
-        if sub == 0:
-            maty_wait(1, 3)
-            maty_relay(1).start()
 
     def relay(sub):
         for way in range(2):
-            ring_copy(way, sub).wait_recv()
+            ring_copy(way, sub, way).wait_recv()
             start(relay_copy(way, sub))
+        for way in range(2):
+            ring_copy(way, sub, 1 - way).wait_recv()
             start(core_copy(1 + way, sub))
 
     def far(sub):
@@ -520,19 +519,32 @@
         else:
             place_tile(held[place], result, xh, place)
 
+    load_mat.wait()
+    live = counts[0, 0]
+    for k in range(8):
+        wide[0, :, k * 256 : k * 256 + 256] = own_mat[k] * jnp.where(k < live, 1.0, 0.0).astype(BF16)
+
     for sub in range(SUBS):
         core_wait(0, sub)
         product(0, sub, 0)
-    relay(0)
     info_copy.wait()
     listed = pltpu.make_async_copy(info_got, info_s, local_sem.at[2])
     listed.start()
     listed.wait()
+    other_live = info_s[1, 0]
+
+    def widen(piece, step):
+        p_far = ((y + 4 - step) % 4) * 2 + xl
+        k = (p_far + 1 - 2 * (p_far % 2), p_far)[piece]
+        where = pl.ds(pl.multiple_of(k * 256, 256), 256)
+        wide[1, :, where] = other_mat[k] * jnp.where(k < other_live, 1.0, 0.0).astype(BF16)
+
+    for piece, step in ((0, 0), (1, 0), (0, 1), (1, 3)):
+        widen(piece, step)
+    relay(0)
     for piece, step in ((0, 3), (0, 2), (1, 1), (1, 2)):
         maty_wait(piece, step)
-    other_live = info_s[1, 0]
-    for k in range(8):
-        wide[1, :, k * 256 : k * 256 + 256] = other_mat[k] * jnp.where(k < other_live, 1.0, 0.0).astype(BF16)
+        widen(piece, step)
     product(0, 0, 1)
     product(0, 1, 1)
 
@@ -624,7 +636,7 @@
         dma((4,)), dma((4,)),
         dma((16,)), dma((16,)),
         dma((8,)), dma((8,)),
-        dma((4,)), dma((4,)),
+        dma((4, 2)), dma((4, 2)),
         dma((4,)), dma((4,)),
         dma((10,)), dma((10,)),
         dma((8,)), dma((8,)),

time: 90.6 us -> 90.7 us (level)
  no operation moved by 1% of the time
where the time goes in v5:
time: 90.7 us; the launch traced here: 89 us
  Pallas kernels  86.4 us (95%)
  local copies, waits for them, and re-layouts  2.02 us (2%)
    pallas_call x1, Pallas kernels, shards(): pl.pallas_call(kernel, out_shape=pltpu.VMEM((2, 512, 1024), F32), in_spec...  86.4 us
    unnamed x1, local copies, waits for them, and re-layouts  2.02 us

profile of v5, /device:TPU:1, one launch (start us, length us, event | category | flops | bytes accessed | tf_op | source)
XLA Modules:
  0.0 89.0 jit_solution(6109276912264533098)
XLA Ops:
  0.7 86.4 %shard_map.91 = f32[2,512,1024]{2,1,0:T(8,128)S(1)} custom-call(f32[2,256,1024]{2,1,0:T(8,128)} %child_h.1, f32[4,2,4,256]{3,2,1,0:T(4,128)} %taps.1, s32[4,2,256]{2,1,0:T(2,128)} %bands.1, f32[4,2,256]{2,1,0:T(2,128)} %shifts.1, f32[4,2,256]{2,1,0:T(2,128)} %bases.1, f32[4,2,256]{2,1,0:T(2,128)} %slopes.1, s32[1,8]{1,0:T(1,128)} %sources.1, ...), custom_call_target="tpu_custom_call" | custom-call | tf_op jit(solution)/shard_map/pallas_call | solution.py:646
  87.0 2.0 %copy.11 = f32[2,512,1024]{2,1,0:T(8,128)} copy(f32[2,512,1024]{2,1,0:T(8,128)S(1)} %shard_map.91) | data formatting | bytes 8388608
